TPU v7x, 128 devices: a whole 4x4x4 slice. The times are simulated.
128 devices in a mesh: tm: 32 (over z, x, y_hi), rows: 4 (over y_lo, core).
Axes of the slice: x: 4, y: 4 (y_hi: 2, y_lo: 2; y = y_hi * 2 + y_lo), z: 4, core: 2. Of those that a mesh axis runs over, the one named last changes fastest.
Arguments:
- video: bfloat16 [256, 32, 128, 128], P('tm', 'rows'), may hold values from -36 to 50
- conv_weight: bfloat16 [3, 3, 3, 128, 256], replicated, may hold values from -0.109375 to 0.109375
- norm_gain: float32 [256], replicated, may hold values from 0.5 to 1.5
- norm_bias: float32 [256], replicated, may hold values from -3 to 3
Outputs:
- patch_tokens: bfloat16 [16, 64, 256, 1024], P('rows', 'tm')
All inputs are finite; a program needn't handle non-finite values.
Results may differ from a plain program's by a relative error of at most 0.0049.
Values may be sent and summed in bfloat16 or wider, within the bound.
A program may use at most 128 MiB of HBM per device.

v0:
```python
import jax
import jax.numpy as jnp
from jax import lax
from jax.sharding import PartitionSpec as P

GROUPS = 32
inv_root = 0.7071067811865476


def from_partner(block, axis, distance):
    count = lax.axis_size(axis)
    route = []
    for low in range(count):
        high = low | 1 << distance
        if high != low and high < count:
            route += [(low, high), (high, low)]
    return lax.ppermute(block, axis, route)


def shifted(block, axis, distance):
    devices = range(lax.axis_size(axis))
    route = [(i - distance, i) for i in devices if i - distance in devices]
    return lax.ppermute(block, axis, route)


def padded_2(cells, sides, width):
    for axis, dim in sides:
        count = lax.axis_size(axis)
        ends = count - 1
        head = lax.slice_in_dim(cells, 0, width, axis=dim)
        tail = lax.slice_in_dim(cells, cells.shape[dim] - width, cells.shape[dim], axis=dim)
        cells = jnp.concatenate(
            [
                lax.ppermute(tail, axis, [(i, (i + 1) % count) for i in range(ends)]),
                cells,
                lax.ppermute(head, axis, [((i + 1) % count, i) for i in range(ends)]),
            ],
            axis=dim,
        )
    return cells


def per_device(video, conv_weight, norm_gain, norm_bias):
    frames, height, width, channels = video.shape
    tm_count = lax.axis_size("tm")
    current = video.astype(jnp.float32)
    position = lax.axis_index("tm")
    for bit_number in range(3):
        partner = from_partner(current, "tm", bit_number)
        is_upper = position >> bit_number & 1 == 1
        current = jnp.where(
            is_upper, (partner - current) * inv_root, (current + partner) * inv_root
        )
    wavelet = current.astype(jnp.bfloat16)
    last_frames = wavelet[frames - 2 :]
    earlier = shifted(last_frames, "tm", 1)
    extended = jnp.concatenate([earlier, wavelet], axis=0)
    with_rows = padded_2(extended, (("rows", 1),), 1)
    padded = jnp.pad(with_rows, ((0, 0), (0, 0), (1, 1), (0, 0)))
    convolved = lax.conv_general_dilated(
        padded[None],
        conv_weight,
        (1, 1, 1),
        "VALID",
        dimension_numbers=("NDHWC", "DHWIO", "NDHWC"),
        preferred_element_type=jnp.float32,
    )[0]
    out_frames, out_height, out_width, out_channels = convolved.shape
    group_count = GROUPS
    groups = convolved.reshape(
        out_frames, out_height, out_width, group_count, out_channels // group_count
    )
    entries = float(
        out_frames
        * out_height
        * out_width
        * (out_channels // group_count)
        * tm_count
        * lax.axis_size("rows")
    )
    local_sums = jnp.sum(groups, axis=(0, 1, 2, 4))
    group_total = lax.psum(local_sums, ("tm", "rows"))
    group_mean = group_total / entries
    centered = groups - group_mean[:, None]
    squares = lax.psum(jnp.sum(centered * centered, axis=(0, 1, 2, 4)), ("tm", "rows"))
    variance = squares / entries
    normed = (centered / jnp.sqrt(variance + 1e-05)[:, None]).reshape(
        out_frames, out_height, out_width, out_channels
    )
    activated = jax.nn.silu(normed * norm_gain + norm_bias).astype(jnp.bfloat16)
    arranged = activated.reshape(
        out_frames, out_height // 2, 2, out_width // 2, 2, out_channels
    ).transpose(1, 3, 0, 2, 4, 5)
    arranged = arranged.reshape(out_height // 2, out_width // 2, out_frames, 4 * out_channels)
    return lax.all_to_all(arranged, "tm", split_axis=1, concat_axis=2, tiled=True)


def solution(mesh):
    placed = (P("tm", "rows", None, None), P(), P(), P())
    return jax.shard_map(
        per_device,
        mesh=mesh,
        in_specs=placed,
        out_specs=P("rows", "tm", None, None),
        check_vma=False,
    )
```

profile of v0, /device:TPU:0, one launch (start us, length us, event | category | flops | bytes accessed | tf_op | source)
XLA Modules:
  0.0 597.1 jit_solution(17662172223809165032)
XLA Ops:
  0.0 0.0 copy-start
  0.0 4.3 convert_element_type.12
  4.3 3.3 collective-permute-start
  7.5 90.9 %collective-permute-done = f32[8,8,128,128]{3,2,1,0:T(8,128)} collective-permute-done((f32[8,8,128,128]{3,2,1,0:T(8,128)}, f32[8,8,128,128]{3,2,1,0:T(8,128)}, u32[]{:S(2)}, u32[]{:S(2)}) %collective-permute-start) | collective-permute-done | bytes 4194336 | tf_op jit(solution)/shard_map/ppermute | solution.py:17
  98.4 5.9 multiply_select_fusion.1
  104.3 1.5 collective-permute-start.1
  105.9 90.2 %collective-permute-done.1 = f32[8,8,128,128]{3,2,1,0:T(8,128)} collective-permute-done((f32[8,8,128,128]{3,2,1,0:T(8,128)}, f32[8,8,128,128]{3,2,1,0:T(8,128)}, u32[]{:S(2)}, u32[]{:S(2)}) %collective-permute-start.1) | collective-permute-done | bytes 4194336 | tf_op jit(solution)/shard_map/ppermute | solution.py:17
  196.1 6.9 %multiply_select_fusion = f32[8,8,128,128]{3,2,1,0:T(8,128)} fusion(f32[8,8,128,128]{3,2,1,0:T(8,128)} %multiply_select_fusion.1, f32[8,8,128,128]{3,2,1,0:T(8,128)} %collective-permute-done.1, pred[]{:T(512)S(6)} %eq.10), kind=kLoop, calls=%fused_computation.15 | loop fusion | flops 5242880 | bytes 12582913 | tf_op jit(solution)/shard_map/jit(_where)/select_n | solution.py:51
  203.0 3.0 collective-permute-start.2
  206.1 89.3 %collective-permute-done.2 = f32[8,8,128,128]{3,2,1,0:T(8,128)} collective-permute-done((f32[8,8,128,128]{3,2,1,0:T(8,128)}, f32[8,8,128,128]{3,2,1,0:T(8,128)}, u32[]{:S(2)}, u32[]{:S(2)}) %collective-permute-start.2) | collective-permute-done | bytes 4194336 | tf_op jit(solution)/shard_map/ppermute | solution.py:17
  295.4 4.5 select_convert_fusion
  299.9 5.1 collective-permute-start.3
  305.1 8.4 %collective-permute-done.3 = bf16[2,8,128,128]{3,2,1,0:T(8,128)(2,1)S(1)} collective-permute-done((bf16[2,8,128,128]{3,2,1,0:T(8,128)(2,1)S(1)}, bf16[2,8,128,128]{3,2,1,0:T(8,128)(2,1)S(1)}, u32[]{:S(2)}, u32[]{:S(2)}) %collective-permute-start.3) | collective-permute-done | bytes 524320 | tf_op jit(solution)/shard_map/ppermute | solution.py:23
  313.5 0.1 pad_maximum_fusion.1
  313.5 1.3 collective-permute-start.4
  314.9 1.3 collective-permute-start.5
  316.2 0.0 collective-permute-done.4
  316.2 3.1 collective-permute-done.5
  319.3 2.1 fusion.13
  321.4 2.0 pad.5
  323.4 6.9 %reshape.19 = bf16[10,10,1,8,17,128]{5,4,3,1,0,2:T(8,128)(2,1)} reshape(bf16[10,10,1,136,128]{4,3,1,0,2:T(8,128)(2,1)} %pad.5) | data formatting | bytes 6963200 | tf_op jit(solution)/shard_map/conv_general_dilated | solution.py:60
  330.4 3.0 copy.29
  333.4 0.1 slice.15
  333.5 0.0 copy-done
  333.5 0.0 copy-done.3
  333.5 19.0 %select_reduce_fusion.1 = (f32[256]{0:T(256)S(1)}, f32[8,8,8,17,256]{4,2,3,1,0:T(8,128)}) fusion(pred[8,17]{0,1:T(8,128)(4,1)S(1)} %copy-done.3, bf16[3,3,3,128,256]{4,3,2,1,0:T(8,128)(2,1)S(1)} %copy-done, bf16[10,10,1,7,2,128]{5,3,4,1,0,2:T(8,128)(2,1)S(1)} %slice.15, bf16[10,10,1,8,17,128]{5,3,4,1,0,2:T(8,128)(2,1)S(1)} %copy.29), kind=kOutput, calls=%fused_computation.3 | convolution fusion | flops 15419842560 | bytes 14523528 | tf_op jit(solution)/shard_map/conv_general_dilated | solution.py:60
  352.6 0.1 reduce_sum.24
  352.7 0.1 reduce_sum.25
  352.8 75.9 %psum.14 = f32[32]{0:T(128)S(1)} all-reduce(f32[32]{0:T(128)S(1)} %reduce_sum.25), channel_id=1, replica_groups=mesh['tm'=32,'rows'=4] {'tm','rows'}, use_global_device_ids=true, to_apply=%region_2.3 | all-reduce | flops 32 | bytes 256 | tf_op jit(solution)/shard_map/psum | solution.py:82
  428.7 0.1 sub.31
  428.8 0.1 sub.32
  428.8 0.0 copy-start.2
  428.9 6.3 %copy.30 = f32[8,8,8,17,256]{4,1,3,2,0:T(8,128)S(1)} copy(f32[8,8,8,17,256]{4,2,3,1,0:T(8,128)} %get-tuple-element.8) | data formatting | bytes 17825792 | tf_op jit(solution)/shard_map/conv_general_dilated | solution.py:60
  435.2 1.5 select_reduce_fusion
  436.8 4.1 slice.16
  440.8 0.1 reduce_sum.36
  440.9 0.1 reduce_sum.37
  441.0 0.0 copy-start.4
  441.0 0.0 copy-start.5
  441.0 11.5 %copy.31 = f32[8,8,1,128,256]{4,0,3,1,2:T(8,128)} copy(f32[8,8,1,128,256]{4,1,3,0,2:T(8,128)} %slice.16) | data formatting | bytes 16777216 | tf_op jit(solution)/shard_map/conv_general_dilated | solution.py:60
  452.5 62.4 %psum.15 = f32[32]{0:T(128)S(1)} all-reduce(f32[32]{0:T(128)S(1)} %reduce_sum.37), channel_id=1, replica_groups=mesh['tm'=32,'rows'=4] {'tm','rows'}, use_global_device_ids=true, to_apply=%region_5.6 | all-reduce | flops 32 | bytes 256 | tf_op jit(solution)/shard_map/psum | solution.py:85
  515.0 0.1 div.27
  515.0 0.1 div.28
  515.2 6.9 %fusion.5 = bf16[4,64,8,2,2,256]{5,1,4,3,0,2:T(8,128)(2,1)S(1)} fusion(f32[256]{0:T(256)S(1)} %copy-done.4, f32[256]{0:T(256)S(1)} %copy-done.5, f32[256]{0:T(256)S(1)} %div.28, f32[256]{0:T(256)S(1)} %sub.32, f32[8,4,2,64,2,256]{5,0,4,3,2,1:T(8,128)} %bitcast.27), kind=kLoop, calls=%fused_computation.17 | loop fusion | flops 18874368 | bytes 12587008 | tf_op jit(solution)/shard_map/transpose | solution.py:93
  522.0 6.4 %copy.37 = bf16[4,64,8,2,2,256]{5,4,3,2,0,1:T(2,128)(2,1)} copy(bf16[4,64,8,2,2,256]{5,1,4,3,0,2:T(8,128)(2,1)S(1)} %fusion.5) | data formatting | bytes 8388608 | tf_op jit(solution)/shard_map/reshape | solution.py:94
  528.4 7.7 %reshape.33 = bf16[4,64,8,1024]{3,2,0,1:T(8,128)(2,1)} reshape(bf16[4,64,8,2,2,256]{5,4,3,2,0,1:T(2,128)(2,1)} %copy.37) | data formatting | bytes 8388608 | tf_op jit(solution)/shard_map/reshape | solution.py:94
  536.1 58.5 %all_to_all.18 = bf16[4,64,8,1024]{3,2,0,1:T(8,128)(2,1)S(1)} all-to-all(bf16[4,64,8,1024]{3,2,0,1:T(8,128)(2,1)} %reshape.33), channel_id=1, replica_groups=mesh['tm'=32,'rows'=4] {'tm'}, dimensions={1} | all-to-all | bytes 8388608 | tf_op jit(solution)/shard_map/all_to_all | solution.py:95
  594.6 2.5 copy.52
  (9 shorter events, 0.1 us)
Async XLA Ops:
  0.0 333.5 %copy-start = (bf16[3,3,3,128,256]{4,3,2,1,0:T(8,128)(2,1)S(1)}, bf16[3,3,3,128,256]{4,3,2,1,0:T(8,128)(2,1)}, u32[]{:S(2)}) copy-start(bf16[3,3,3,128,256]{4,3,2,1,0:T(8,128)(2,1)} %param.5) | copy-start | bytes 5308420
  4.3 94.2 %collective-permute-start = (f32[8,8,128,128]{3,2,1,0:T(8,128)}, f32[8,8,128,128]{3,2,1,0:T(8,128)}, u32[]{:S(2)}, u32[]{:S(2)}) collective-permute-start(f32[8,8,128,128]{3,2,1,0:T(8,128)} %convert_element_type.12), channel_id=1, source_target_pairs={{0,4},{4,0},{8,12},{12,8},{16,20},{20,16},{24,28},{28,24},{32,36},... | collective-permute-start | bytes 12582920 | tf_op jit(solution)/shard_map/ppermute | solution.py:17
  104.3 91.8 %collective-permute-start.1 = (f32[8,8,128,128]{3,2,1,0:T(8,128)}, f32[8,8,128,128]{3,2,1,0:T(8,128)}, u32[]{:S(2)}, u32[]{:S(2)}) collective-permute-start(f32[8,8,128,128]{3,2,1,0:T(8,128)} %multiply_select_fusion.1), channel_id=1, source_target_pairs={{0,8},{8,0},{4,12},{12,4},{16,24},{24,16},{20,28},{28,20},{32,40},... | collective-permute-start | bytes 12582920 | tf_op jit(solution)/shard_map/ppermute | solution.py:17
  203.0 92.4 %collective-permute-start.2 = (f32[8,8,128,128]{3,2,1,0:T(8,128)}, f32[8,8,128,128]{3,2,1,0:T(8,128)}, u32[]{:S(2)}, u32[]{:S(2)}) collective-permute-start(f32[8,8,128,128]{3,2,1,0:T(8,128)} %multiply_select_fusion), channel_id=1, source_target_pairs={{0,16},{16,0},{4,20},{20,4},{8,24},{24,8},{12,28},{28,12},{32,48},... | collective-permute-start | bytes 12582920 | tf_op jit(solution)/shard_map/ppermute | solution.py:17
  299.9 13.5 %collective-permute-start.3 = (bf16[2,8,128,128]{3,2,1,0:T(8,128)(2,1)S(1)}, bf16[2,8,128,128]{3,2,1,0:T(8,128)(2,1)S(1)}, u32[]{:S(2)}, u32[]{:S(2)}) collective-permute-start(bf16[2,8,128,128]{3,2,1,0:T(8,128)(2,1)S(1)} %slice.14), channel_id=1, source_target_pairs={{0,4},{4,8},{8,12},{12,16},{16,20},{20,24},{24,28},{28,32},{32,36}... | collective-permute-start | bytes 1572872 | tf_op jit(solution)/shard_map/ppermute | solution.py:23
  313.5 2.6 collective-permute-start.4
  314.9 4.4 collective-permute-start.5
  330.4 3.2 copy-start.3
  428.8 6.4 %copy-start.2 = (f32[8,8,8,17,256]{4,2,3,1,0:T(8,128)S(1)}, f32[8,8,8,17,256]{4,2,3,1,0:T(8,128)}, u32[]{:S(2)}) copy-start(f32[8,8,8,17,256]{4,2,3,1,0:T(8,128)} %get-tuple-element.8) | copy-start | bytes 26738692
  441.0 74.1 %copy-start.4 = (f32[256]{0:T(256)S(1)}, f32[256]{0:T(256)}, u32[]{:S(2)}) copy-start(f32[256]{0:T(256)} %param.7) | copy-start | bytes 3076
  441.0 74.1 %copy-start.5 = (f32[256]{0:T(256)S(1)}, f32[256]{0:T(256)}, u32[]{:S(2)}) copy-start(f32[256]{0:T(256)} %param.6) | copy-start | bytes 3076
  594.6 2.5 copy-start.1
where the time goes:
time: 598 us; the launch traced here: 597 us
  waiting for transfers between devices  282 us (47%)
  blocking collectives  197 us (33%)
  local copies, waits for them, and re-layouts  51 us (9%)
  other arithmetic  32.4 us (5%)
  matrix products  19 us (3%)
  starting transfers between devices  15.6 us (3%)
    ppermute x3, waiting for transfers between devices, from_partner(): return lax.ppermute(block, axis, route)  270 us
    psum x1, blocking collectives, per_device(): group_total = lax.psum(local_sums, ('tm', 'rows'))  75.9 us
    psum x1, blocking collectives, per_device(): lax.psum(jnp.sum(centered * centered, axis=(0, 1, 2, 4)), ('tm', 'rows'))  62.4 us
    all_to_all x1, blocking collectives, per_device(): lax.all_to_all(arranged, 'tm', split_axis=1, concat_axis=2, tiled=True)  58.5 us
    conv_general_dilated x6, local copies, waits for them, and re-layouts, per_device(): lax.conv_general_dilated(padded[None], conv_weight, (1, 1, 1), 'VALID', d...  31.9 us
    conv_general_dilated x1, matrix products, per_device(): lax.conv_general_dilated(padded[None], conv_weight, (1, 1, 1), 'VALID', d...  19 us
    reshape x2, local copies, waits for them, and re-layouts, per_device(): arranged.reshape(out_height // 2, out_width // 2, out_frames, 4 * out_cha...  14.1 us
    select_n x2, other arithmetic, per_device(): jnp.where(is_upper, (partner - current) * inv_root, (current + partner) *...  12.8 us
  transfers between devices with their start and end apart: 6, of which 5 were waited for; matrix products, arithmetic and copies ran while one was open for 0% of the time, Pallas kernels for 0%

commit v1 on v0

--- a/solution.py
+++ b/solution.py
@@ -79,7 +79,8 @@
         * lax.axis_size("rows")
     )
     local_sums = jnp.sum(groups, axis=(0, 1, 2, 4))
-    group_total = lax.psum(local_sums, ("tm", "rows"))
+    far_arr = lax.psum(local_sums, "tm")
+    group_total = lax.psum(far_arr, "rows")
     group_mean = group_total / entries
     centered = groups - group_mean[:, None]
     squares = lax.psum(jnp.sum(centered * centered, axis=(0, 1, 2, 4)), ("tm", "rows"))

time: 598 us -> 630 us (1.054)
  blocking collectives: 197 us -> 229 us
    psum x1 -> x2, blocking collectives: 75.9 us -> 107 us  [the longest x1 99.1 us: per_device(): far_arr = lax.psum(local_sums, 'tm')]
where the time goes in v1:
time: 630 us; the launch traced here: 629 us
  waiting for transfers between devices  282 us (45%)
  blocking collectives  229 us (36%)
  local copies, waits for them, and re-layouts  51 us (8%)
  other arithmetic  32.4 us (5%)
  matrix products  19 us (3%)
  starting transfers between devices  15.6 us (2%)
    ppermute x3, waiting for transfers between devices, from_partner(): return lax.ppermute(block, axis, route)  270 us
    psum x1, blocking collectives, per_device(): far_arr = lax.psum(local_sums, 'tm')  99.1 us
    psum x1, blocking collectives, per_device(): lax.psum(jnp.sum(centered * centered, axis=(0, 1, 2, 4)), ('tm', 'rows'))  63.5 us
    all_to_all x1, blocking collectives, per_device(): lax.all_to_all(arranged, 'tm', split_axis=1, concat_axis=2, tiled=True)  58.5 us
    conv_general_dilated x6, local copies, waits for them, and re-layouts, per_device(): lax.conv_general_dilated(padded[None], conv_weight, (1, 1, 1), 'VALID', d...  31.9 us
    conv_general_dilated x1, matrix products, per_device(): lax.conv_general_dilated(padded[None], conv_weight, (1, 1, 1), 'VALID', d...  19 us
    reshape x2, local copies, waits for them, and re-layouts, per_device(): arranged.reshape(out_height // 2, out_width // 2, out_frames, 4 * out_cha...  14.1 us
    select_n x2, other arithmetic, per_device(): jnp.where(is_upper, (partner - current) * inv_root, (current + partner) *...  12.8 us
  transfers between devices with their start and end apart: 6, of which 5 were waited for; matrix products, arithmetic and copies ran while one was open for 0% of the time, Pallas kernels for 0%

profile of v1, /device:TPU:0, one launch (start us, length us, event | category | flops | bytes accessed | tf_op | source)
XLA Modules:
  0.0 629.5 jit_solution(13479316300600433015)
XLA Ops:
  0.0 0.0 copy-start
  0.0 4.3 convert_element_type.12
  4.3 3.3 collective-permute-start
  7.5 90.9 %collective-permute-done = f32[8,8,128,128]{3,2,1,0:T(8,128)} collective-permute-done((f32[8,8,128,128]{3,2,1,0:T(8,128)}, f32[8,8,128,128]{3,2,1,0:T(8,128)}, u32[]{:S(2)}, u32[]{:S(2)}) %collective-permute-start) | collective-permute-done | bytes 4194336 | tf_op jit(solution)/shard_map/ppermute | solution.py:17
  98.4 5.9 multiply_select_fusion.1
  104.3 1.5 collective-permute-start.1
  105.9 90.2 %collective-permute-done.1 = f32[8,8,128,128]{3,2,1,0:T(8,128)} collective-permute-done((f32[8,8,128,128]{3,2,1,0:T(8,128)}, f32[8,8,128,128]{3,2,1,0:T(8,128)}, u32[]{:S(2)}, u32[]{:S(2)}) %collective-permute-start.1) | collective-permute-done | bytes 4194336 | tf_op jit(solution)/shard_map/ppermute | solution.py:17
  196.1 6.9 %multiply_select_fusion = f32[8,8,128,128]{3,2,1,0:T(8,128)} fusion(f32[8,8,128,128]{3,2,1,0:T(8,128)} %multiply_select_fusion.1, f32[8,8,128,128]{3,2,1,0:T(8,128)} %collective-permute-done.1, pred[]{:T(512)S(6)} %eq.10), kind=kLoop, calls=%fused_computation.15 | loop fusion | flops 5242880 | bytes 12582913 | tf_op jit(solution)/shard_map/jit(_where)/select_n | solution.py:51
  203.0 3.0 collective-permute-start.2
  206.1 89.3 %collective-permute-done.2 = f32[8,8,128,128]{3,2,1,0:T(8,128)} collective-permute-done((f32[8,8,128,128]{3,2,1,0:T(8,128)}, f32[8,8,128,128]{3,2,1,0:T(8,128)}, u32[]{:S(2)}, u32[]{:S(2)}) %collective-permute-start.2) | collective-permute-done | bytes 4194336 | tf_op jit(solution)/shard_map/ppermute | solution.py:17
  295.4 4.5 select_convert_fusion
  299.9 5.1 collective-permute-start.3
  305.1 8.4 %collective-permute-done.3 = bf16[2,8,128,128]{3,2,1,0:T(8,128)(2,1)S(1)} collective-permute-done((bf16[2,8,128,128]{3,2,1,0:T(8,128)(2,1)S(1)}, bf16[2,8,128,128]{3,2,1,0:T(8,128)(2,1)S(1)}, u32[]{:S(2)}, u32[]{:S(2)}) %collective-permute-start.3) | collective-permute-done | bytes 524320 | tf_op jit(solution)/shard_map/ppermute | solution.py:23
  313.5 0.1 pad_maximum_fusion.1
  313.5 1.3 collective-permute-start.4
  314.9 1.3 collective-permute-start.5
  316.2 0.0 collective-permute-done.4
  316.2 3.1 collective-permute-done.5
  319.3 2.1 fusion.13
  321.4 2.0 pad.5
  323.4 6.9 %reshape.19 = bf16[10,10,1,8,17,128]{5,4,3,1,0,2:T(8,128)(2,1)} reshape(bf16[10,10,1,136,128]{4,3,1,0,2:T(8,128)(2,1)} %pad.5) | data formatting | bytes 6963200 | tf_op jit(solution)/shard_map/conv_general_dilated | solution.py:60
  330.4 3.0 copy.29
  333.4 0.1 slice.15
  333.5 0.0 copy-done
  333.5 19.0 %select_reduce_fusion.1 = (f32[256]{0:T(256)S(1)}, f32[8,8,8,17,256]{4,2,3,1,0:T(8,128)}) fusion(pred[8,17]{0,1:T(8,128)(4,1)S(1)} %copy-done.3, bf16[3,3,3,128,256]{4,3,2,1,0:T(8,128)(2,1)S(1)} %copy-done, bf16[10,10,1,7,2,128]{5,3,4,1,0,2:T(8,128)(2,1)S(1)} %slice.15, bf16[10,10,1,8,17,128]{5,3,4,1,0,2:T(8,128)(2,1)S(1)} %copy.29), kind=kOutput, calls=%fused_computation.3 | convolution fusion | flops 15419842560 | bytes 14523528 | tf_op jit(solution)/shard_map/conv_general_dilated | solution.py:60
  352.6 0.1 reduce_sum.24
  352.7 0.1 reduce_sum.25
  352.8 99.1 %psum.21 = f32[32]{0:T(128)S(1)} all-reduce(f32[32]{0:T(128)S(1)} %reduce_sum.25), channel_id=1, replica_groups=mesh['tm'=32,'rows'=4] {'tm'}, use_global_device_ids=true, to_apply=%region_2.3 | all-reduce | flops 32 | bytes 256 | tf_op jit(solution)/shard_map/psum | solution.py:82
  451.9 8.2 %psum.22 = f32[32]{0:T(128)S(1)} all-reduce(f32[32]{0:T(128)S(1)} %psum.21), channel_id=1, replica_groups=mesh['tm'=32,'rows'=4] {'rows'}, use_global_device_ids=true, to_apply=%region_3.4 | all-reduce | flops 32 | bytes 256 | tf_op jit(solution)/shard_map/psum | solution.py:83
  460.1 0.1 sub.31
  460.2 0.1 sub.32
  460.3 6.3 %copy.30 = f32[8,8,8,17,256]{4,1,3,2,0:T(8,128)S(1)} copy(f32[8,8,8,17,256]{4,2,3,1,0:T(8,128)} %get-tuple-element.8) | data formatting | bytes 17825792 | tf_op jit(solution)/shard_map/conv_general_dilated | solution.py:60
  466.6 0.0 copy-done.2
  466.6 1.5 select_reduce_fusion
  468.2 4.1 slice.16
  472.2 0.1 reduce_sum.36
  472.3 0.1 reduce_sum.37
  472.4 0.0 copy-start.4
  472.5 0.0 copy-start.5
  472.5 11.5 %copy.31 = f32[8,8,1,128,256]{4,0,3,1,2:T(8,128)} copy(f32[8,8,1,128,256]{4,1,3,0,2:T(8,128)} %slice.16) | data formatting | bytes 16777216 | tf_op jit(solution)/shard_map/conv_general_dilated | solution.py:60
  483.9 63.5 %psum.23 = f32[32]{0:T(128)S(1)} all-reduce(f32[32]{0:T(128)S(1)} %reduce_sum.37), channel_id=1, replica_groups=mesh['tm'=32,'rows'=4] {'tm','rows'}, use_global_device_ids=true, to_apply=%region_6.7 | all-reduce | flops 32 | bytes 256 | tf_op jit(solution)/shard_map/psum | solution.py:86
  547.4 0.1 div.27
  547.5 0.1 div.28
  547.6 6.9 %fusion.5 = bf16[4,64,8,2,2,256]{5,1,4,3,0,2:T(8,128)(2,1)S(1)} fusion(f32[256]{0:T(256)S(1)} %copy-done.4, f32[256]{0:T(256)S(1)} %copy-done.5, f32[256]{0:T(256)S(1)} %div.28, f32[256]{0:T(256)S(1)} %sub.32, f32[8,4,2,64,2,256]{5,0,4,3,2,1:T(8,128)} %bitcast.27), kind=kLoop, calls=%fused_computation.17 | loop fusion | flops 18874368 | bytes 12587008 | tf_op jit(solution)/shard_map/transpose | solution.py:94
  554.5 6.4 %copy.37 = bf16[4,64,8,2,2,256]{5,4,3,2,0,1:T(2,128)(2,1)} copy(bf16[4,64,8,2,2,256]{5,1,4,3,0,2:T(8,128)(2,1)S(1)} %fusion.5) | data formatting | bytes 8388608 | tf_op jit(solution)/shard_map/reshape | solution.py:95
  560.8 7.7 %reshape.33 = bf16[4,64,8,1024]{3,2,0,1:T(8,128)(2,1)} reshape(bf16[4,64,8,2,2,256]{5,4,3,2,0,1:T(2,128)(2,1)} %copy.37) | data formatting | bytes 8388608 | tf_op jit(solution)/shard_map/reshape | solution.py:95
  568.5 58.5 %all_to_all.18 = bf16[4,64,8,1024]{3,2,0,1:T(8,128)(2,1)S(1)} all-to-all(bf16[4,64,8,1024]{3,2,0,1:T(8,128)(2,1)} %reshape.33), channel_id=1, replica_groups=mesh['tm'=32,'rows'=4] {'tm'}, dimensions={1} | all-to-all | bytes 8388608 | tf_op jit(solution)/shard_map/all_to_all | solution.py:96
  627.0 2.5 copy.52
  (10 shorter events, 0.1 us)
Async XLA Ops:
  0.0 333.5 %copy-start = (bf16[3,3,3,128,256]{4,3,2,1,0:T(8,128)(2,1)S(1)}, bf16[3,3,3,128,256]{4,3,2,1,0:T(8,128)(2,1)}, u32[]{:S(2)}) copy-start(bf16[3,3,3,128,256]{4,3,2,1,0:T(8,128)(2,1)} %param.5) | copy-start | bytes 5308420
  4.3 94.2 %collective-permute-start = (f32[8,8,128,128]{3,2,1,0:T(8,128)}, f32[8,8,128,128]{3,2,1,0:T(8,128)}, u32[]{:S(2)}, u32[]{:S(2)}) collective-permute-start(f32[8,8,128,128]{3,2,1,0:T(8,128)} %convert_element_type.12), channel_id=1, source_target_pairs={{0,4},{4,0},{8,12},{12,8},{16,20},{20,16},{24,28},{28,24},{32,36},... | collective-permute-start | bytes 12582920 | tf_op jit(solution)/shard_map/ppermute | solution.py:17
  104.3 91.8 %collective-permute-start.1 = (f32[8,8,128,128]{3,2,1,0:T(8,128)}, f32[8,8,128,128]{3,2,1,0:T(8,128)}, u32[]{:S(2)}, u32[]{:S(2)}) collective-permute-start(f32[8,8,128,128]{3,2,1,0:T(8,128)} %multiply_select_fusion.1), channel_id=1, source_target_pairs={{0,8},{8,0},{4,12},{12,4},{16,24},{24,16},{20,28},{28,20},{32,40},... | collective-permute-start | bytes 12582920 | tf_op jit(solution)/shard_map/ppermute | solution.py:17
  203.0 92.4 %collective-permute-start.2 = (f32[8,8,128,128]{3,2,1,0:T(8,128)}, f32[8,8,128,128]{3,2,1,0:T(8,128)}, u32[]{:S(2)}, u32[]{:S(2)}) collective-permute-start(f32[8,8,128,128]{3,2,1,0:T(8,128)} %multiply_select_fusion), channel_id=1, source_target_pairs={{0,16},{16,0},{4,20},{20,4},{8,24},{24,8},{12,28},{28,12},{32,48},... | collective-permute-start | bytes 12582920 | tf_op jit(solution)/shard_map/ppermute | solution.py:17
  299.9 13.5 %collective-permute-start.3 = (bf16[2,8,128,128]{3,2,1,0:T(8,128)(2,1)S(1)}, bf16[2,8,128,128]{3,2,1,0:T(8,128)(2,1)S(1)}, u32[]{:S(2)}, u32[]{:S(2)}) collective-permute-start(bf16[2,8,128,128]{3,2,1,0:T(8,128)(2,1)S(1)} %slice.14), channel_id=1, source_target_pairs={{0,4},{4,8},{8,12},{12,16},{16,20},{20,24},{24,28},{28,32},{32,36}... | collective-permute-start | bytes 1572872 | tf_op jit(solution)/shard_map/ppermute | solution.py:23
  313.5 2.6 collective-permute-start.4
  314.9 4.4 collective-permute-start.5
  330.4 3.2 copy-start.3
  460.3 6.4 %copy-start.2 = (f32[8,8,8,17,256]{4,2,3,1,0:T(8,128)S(1)}, f32[8,8,8,17,256]{4,2,3,1,0:T(8,128)}, u32[]{:S(2)}) copy-start(f32[8,8,8,17,256]{4,2,3,1,0:T(8,128)} %get-tuple-element.8) | copy-start | bytes 26738692
  472.4 75.1 %copy-start.4 = (f32[256]{0:T(256)S(1)}, f32[256]{0:T(256)}, u32[]{:S(2)}) copy-start(f32[256]{0:T(256)} %param.7) | copy-start | bytes 3076
  472.5 75.1 %copy-start.5 = (f32[256]{0:T(256)S(1)}, f32[256]{0:T(256)}, u32[]{:S(2)}) copy-start(f32[256]{0:T(256)} %param.6) | copy-start | bytes 3076
  627.0 2.5 copy-start.1
